TPU v7x, 32 devices: a whole 2x2x4 slice. The times are simulated.
32 devices in a mesh: sim: 16 (over z, y, x), lens: 2 (over core).
Axes of the slice: x: 2, y: 2, z: 4, core: 2. Of those that a mesh axis runs over, the one named last changes fastest.
Arguments:
- patches: bfloat16 [4096, 2, 2048], P(('sim', 'lens')), may hold values from -6 to 6
- patch_cycle: int32 [4096, 1], P(('sim', 'lens')), may hold values from 0 to 15; in each aligned block of 128 rows (0 to 127, 128 to 255, ...) at most 16 rows name the same one
- patch_block: int32 [4096], P(('sim', 'lens')), may hold values from 0 to 7
- m_values: int32 [32], replicated, may hold values from 0 to 8191, as said below
- shell_weight: float32 [2], replicated, may hold values from 0.5 to 2
- legendre_panel: bfloat16 [32, 32, 8192], P('sim', 'lens'), as said below
- spin2_panel: bfloat16 [32, 32, 8192], P('sim', 'lens'), as said below
Outputs:
- kappa_modes: float32 [32, 2, 32], P('sim', None, 'lens')
- shear_modes: float32 [32, 2, 32], P('sim', None, 'lens')
Inputs may be any that keep to these rules, and one draw needn't show every extreme that they name: `patch_cycle`: among the 128 patches of one device, at most 16 lie on one cycle; some device reaches 16. `m_values`: the 32 orders are distinct; slots 2 d and 2 d + 1 hold m and 8191 - m with m below 4096, and some sim index holds 0 and 8191. legendre_panel[j, g, l] is 0 for l < 128 * (m_values[j] // 128). spin2_panel[j, g, l] is 0 for l < 128 * (m_values[j] // 128).
All inputs are finite; a program needn't handle non-finite values.
Results may differ from a plain program's by a relative error of at most 0.014.
Values may be sent and summed in bfloat16 or wider, within the bound.
No kernel may reach another device: no remote copies, remote signals or barrier semaphores. Data moves between devices by JAX's collectives and lax.ppermute only.
A program may use at most 64 MiB of HBM per device.

v0:
```python
import math

import jax
import jax.numpy as jnp
from jax import lax
from jax.sharding import PartitionSpec as P

NPIX = 16384
BPX = 2048
LMAX = 8192
SHELLS = 2


def base_table(m_values):
    pixel = jnp.arange(BPX, dtype=jnp.int32)
    angle_index = pixel[:, None] * m_values[None, :] % NPIX
    angle = angle_index.astype(jnp.float32) * (2.0 * math.pi / NPIX)
    return jnp.concatenate([jnp.cos(angle), jnp.sin(angle)], axis=1)


def fourier_rows(rows, phase, m_values, table):
    number = rows.shape[0]
    flat = rows.astype(jnp.float32).reshape(number * SHELLS, BPX)
    sums = jnp.dot(flat, table, precision=lax.Precision.HIGHEST).reshape(number, SHELLS, 2, -1)
    cosine_part = sums[:, :, 0]
    sine_part = sums[:, :, 1]
    turn_index = phase[:, None] * m_values[None, :] % (2 * NPIX)
    turn = turn_index.astype(jnp.float32) * (math.pi / NPIX)
    turn_cos = jnp.cos(turn)[:, None, :]
    turn_sin = jnp.sin(turn)[:, None, :]
    real_part = turn_cos * cosine_part - turn_sin * sine_part
    imag_part = -(turn_sin * cosine_part + turn_cos * sine_part)
    return jnp.stack([real_part, imag_part], axis=2) / math.sqrt(NPIX)


def on_device(
    patches, patch_cycle, patch_block, m_values, shell_weight, legendre_panel, spin2_panel
):
    n_sim = lax.axis_size("sim")
    n_lens = lax.axis_size("lens")
    lens_rank = lax.axis_index("lens")
    number = patches.shape[0]
    m_dev = legendre_panel.shape[0]
    table = base_table(m_values)
    destination = patch_cycle[:, 0]
    parity = (lens_rank * n_sim + destination) % 2
    phase = 2 * patch_block * BPX + parity
    modes = fourier_rows(patches, phase, m_values, table)
    cycle_onehot = (destination[:, None] == jnp.arange(n_sim, dtype=jnp.int32)[None, :]).astype(
        jnp.float32
    )
    terms = jnp.dot(cycle_onehot.T, modes.reshape(number, -1), precision=lax.Precision.HIGHEST)
    terms = terms.reshape(n_sim, SHELLS * 2, -1)
    summed = lax.psum_scatter(terms, "sim", scatter_dimension=2, tiled=True)
    local_modes = summed.astype(jnp.bfloat16)
    delta = jnp.einsum(
        "rxj,jrl->jxl", local_modes, legendre_panel, preferred_element_type=jnp.float32
    )
    delta = delta.reshape(m_dev, SHELLS, 2, LMAX)
    partial_kappa = jnp.zeros((m_dev, 2, LMAX), jnp.float32)
    for shell in range(SHELLS):
        partial_kappa = partial_kappa + shell_weight[shell] * delta[:, shell]
    partial_kappa = partial_kappa / math.sqrt(n_sim * n_lens)
    kappa = lax.psum(partial_kappa.astype(jnp.bfloat16), "lens").astype(jnp.float32)
    ell = jnp.arange(LMAX, dtype=jnp.int32).astype(jnp.float32)
    factor = jnp.where(
        ell >= 2.0, jnp.sqrt((ell + 2.0) * (ell - 1.0) / jnp.maximum(ell * (ell + 1.0), 1.0)), 0.0
    )
    shear = kappa * factor
    kappa_rounded = kappa.astype(jnp.bfloat16)
    shear_rounded = shear.astype(jnp.bfloat16)
    kappa_modes = jnp.einsum(
        "jcl,jrl->jcr", kappa_rounded, legendre_panel, preferred_element_type=jnp.float32
    )
    shear_modes = jnp.einsum(
        "jcl,jrl->jcr", shear_rounded, spin2_panel, preferred_element_type=jnp.float32
    )
    scale = 1.0 / math.sqrt(LMAX)
    return (kappa_modes * scale, shear_modes * scale)


def solution(mesh):
    placed = (
        P(("sim", "lens"), None, None),
        P(("sim", "lens"), None),
        P(("sim", "lens")),
        P(),
        P(),
        P("sim", "lens", None),
        P("sim", "lens", None),
    )
    return jax.shard_map(
        on_device,
        mesh=mesh,
        in_specs=placed,
        out_specs=(P("sim", None, "lens"), P("sim", None, "lens")),
        check_vma=False,
    )
```

profile of v0, /device:TPU:0, one launch (start us, length us, event | category | flops | bytes accessed | tf_op | source)
XLA Modules:
  0.0 120.7 jit_solution(4829055841886988475)
XLA Ops:
  7.2 0.0 copy-start
  7.2 0.0 all-reduce.3.cloned.1.call-start
  7.2 0.0 copy-start.1
  7.2 0.7 copy-done.1
  7.9 1.1 fusion.14
  9.0 1.5 %reshape.97 = bf16[256,2048]{1,0:T(8,128)(2,1)S(1)} reshape(bf16[128,2,2048]{2,1,0:T(2,128)(2,1)} %param.7) | data formatting | bytes 2097152 | tf_op jit(solution)/shard_map/reshape | solution.py:23
  10.5 1.1 convolution_bitcast_fusion
  11.6 0.1 copy.22
  11.7 0.2 reshape.98
  11.9 0.2 fusion.36
  12.1 0.1 copy.28
  12.2 0.1 copy.29
  12.2 0.0 copy-start.2
  12.2 0.0 copy-start.4
  12.3 0.7 copy-done.2
  12.9 0.0 copy-done.4
  13.0 0.2 fusion.26
  13.1 0.2 fusion.28
  13.4 78.7 %all-reduce = bf16[16,4,32]{0,1,2:T(4,128)(2,1)S(1)} all-reduce(f32[16,4,32]{0,1,2:T(4,128)S(1)} %copy.25), channel_id=2, replica_groups=mesh['sim'=16,'lens'=2] {'sim'}, use_global_device_ids=true, to_apply=%region_0.1.clone | all-reduce | flops 2048 | bytes 12288
  92.0 0.0 copy-start.7
  92.0 0.7 copy-done.7
  92.7 0.6 dynamic-slice
  93.9 0.0 copy-done
  93.9 0.2 fusion.31
  94.1 0.0 copy-start.3
  94.1 0.2 reshape.99
  94.4 0.4 copy-done.3
  94.8 0.6 fusion.37
  95.4 0.0 copy-start.5
  95.4 2.1 %fusion.17 = bf16[2,2,8192]{2,1,0:T(2,128)(2,1)} fusion(f32[2,2,2,8192]{3,2,1,0:T(2,128)S(1)} %reshape.99, f32[]{:T(128)} %bitcast.7, f32[]{:T(128)} %bitcast), kind=kLoop, calls=%fused_computation.27 | loop fusion | flops 163840 | bytes 327688 | tf_op jit(solution)/shard_map/convert_element_type | solution.py:64
  97.4 0.0 all-reduce.3.cloned.1.call-update
  97.5 13.7 %all-reduce.3.cloned.1.call-done = bf16[2,2,8192]{2,1,0:T(2,128)(2,1)} async-done(((bf16[2,2,8192]{2,1,0:T(2,128)(2,1)}), bf16[2,2,8192]{2,1,0:T(2,128)(2,1)}) %all-reduce.3.cloned.1.call-update) | async-done | bytes 65552 | tf_op jit(solution)/shard_map/psum | solution.py:64
  111.2 0.0 copy-start.6
  111.2 1.8 %convolution_multiply_fusion.1 = f32[2,2,16]{2,1,0:T(2,128)} fusion(bf16[2,2,8192]{2,1,0:T(2,128)(2,1)} %all-reduce.3.cloned.1.call-done, bf16[2,16,8192]{2,1,0:T(8,128)(2,1)S(1)} %copy-done), kind=kOutput, calls=%fused_computation.2 | convolution fusion | flops 1048640 | bytes 590080 | tf_op jit(solution)/shard_map/jcl,jrl->jcr/dot_general | solution.py:72
  113.0 0.0 copy-done.5
  113.0 0.0 copy-done.6
  113.0 0.9 convolution_multiply_fusion
  (5 shorter events, 0.1 us)
Async XLA Ops:
  7.2 86.7 %copy-start = (bf16[2,16,8192]{2,1,0:T(8,128)(2,1)S(1)}, bf16[2,16,8192]{2,1,0:T(8,128)(2,1)}, u32[]{:S(2)}) copy-start(bf16[2,16,8192]{2,1,0:T(8,128)(2,1)} %param.12) | copy-start | bytes 1572868
  7.2 104.0 %all-reduce.3.cloned.1.call-start = ((), (), s32[]{:S(2)}) async-start(), calls=%async_computation | async-start | bytes 131072 | tf_op jit(solution)/shard_map/psum | solution.py:64
  7.2 0.7 copy-start.1
  12.2 0.7 copy-start.2
  12.2 0.7 copy-start.4
  92.0 0.7 copy-start.7
  94.1 0.7 copy-start.3
  95.4 17.6 %copy-start.5 = (bf16[2,16,8192]{2,1,0:T(8,128)(2,1)S(1)}, bf16[2,16,8192]{2,1,0:T(8,128)(2,1)}, u32[]{:S(2)}) copy-start(bf16[2,16,8192]{2,1,0:T(8,128)(2,1)} %param.13) | copy-start | bytes 1572868
  111.2 1.8 %copy-start.6 = (bf16[2,2,8192]{2,1,0:T(2,128)(2,1)S(1)}, bf16[2,2,8192]{2,1,0:T(2,128)(2,1)}, u32[]{:S(2)}) copy-start(bf16[2,2,8192]{2,1,0:T(2,128)(2,1)} %all-reduce.3.cloned.1.call-done) | copy-start | bytes 196612
Sparse Core Ops, SparseCore 0:
  97.6 13.5 all-reduce.2
where the time goes:
time: 121 us
  blocking collectives  78.7 us (65%)
  between operations  14.8 us (12%)
  waiting for transfers between devices  13.7 us (11%)
  local copies, waits for them, and re-layouts  6.02 us (5%)
  matrix products  4.13 us (3%)
  other arithmetic  3.37 us (3%)
    unnamed x1, blocking collectives  78.7 us
    psum x1, waiting for transfers between devices, on_device(): lax.psum(partial_kappa.astype(jnp.bfloat16), 'lens').astype(jnp.float32)  13.7 us
    unnamed x19, local copies, waits for them, and re-layouts  3.23 us
  transfers between devices with their start and end apart: 1, of which 1 were waited for; matrix products, arithmetic and copies ran while one was open for 0% of the time, Pallas kernels for 0%

commit v1 on v0

v1 whole, which is shorter than its diff:
```python
import math

import jax
import jax.numpy as jnp
from jax import lax
from jax.experimental import pallas as pl
from jax.experimental.pallas import tpu as pltpu
from jax.sharding import PartitionSpec as P

NPIX = 16384
NT = (((1,), (1,)), ((), ()))


def cos_sin(index, turn):
    quarter = turn // 4
    quadrant = (index + quarter // 2) // quarter
    r = (index - quadrant * quarter).astype(jnp.float32) * (2.0 * math.pi / turn)
    q = r * r
    sine = r + r * q * (-1.0 / 6 + q * (1.0 / 120 + q * (-1.0 / 5040 + q * (1.0 / 362880))))
    cosine = 1.0 + q * (-0.5 + q * (1.0 / 24 + q * (-1.0 / 720 + q * (1.0 / 40320))))
    odd = (quadrant & 1) == 1
    c = jnp.where(odd, sine, cosine)
    s = jnp.where(odd, cosine, sine)
    c = jnp.where(((quadrant + 1) & 2) == 2, -c, c)
    s = jnp.where((quadrant & 2) == 2, -s, s)
    return c, s


def split(x):
    high = x.astype(jnp.bfloat16)
    return high, (x - high.astype(jnp.float32)).astype(jnp.bfloat16)


def iota(shape, dim):
    return lax.broadcasted_iota(jnp.int32, shape, dim)


def terms_kernel(m_ref, cycle_ref, block_ref, patch_ref, out_ref):
    number, shells, bpx = patch_ref.shape
    orders = m_ref.shape[1]
    n_sim = lax.axis_size("sim")
    m_dev = orders // n_sim
    cycles = n_sim * lax.axis_size("lens")
    rank = lax.axis_index("sim")
    square = (orders, orders)
    row = iota(square, 0)
    slot = ((row // m_dev) ^ rank) * m_dev + row % m_dev
    m_row = m_ref[...].astype(jnp.float32)
    m_col = jnp.sum(jnp.where(slot == iota(square, 1), m_row, 0.0), axis=1, keepdims=True)
    m_col = m_col.astype(jnp.int32)
    low_c, low_s = cos_sin((m_col * iota((orders, 128), 1)) & (NPIX - 1), NPIX)
    parts = bpx // 128
    high_c, high_s = cos_sin((m_col * (128 * iota((orders, 128), 1))) & (NPIX - 1), NPIX)
    rows = number * shells
    total = jnp.zeros((4 * orders, rows), jnp.float32)
    for part in range(parts):
        hc = high_c[:, part : part + 1]
        hs = high_s[:, part : part + 1]
        c_high, c_low = split(low_c * hc - low_s * hs)
        s_high, s_low = split(low_s * hc + low_c * hs)
        table = jnp.concatenate([c_high, s_high, c_low, s_low], axis=0)
        chunk = patch_ref[:, :, part * 128 : (part + 1) * 128].reshape(rows, 128)
        total += lax.dot_general(table, chunk, NT, preferred_element_type=jnp.float32)
    total = total[: 2 * orders] + total[2 * orders :]
    cosine, sine = total[:orders], total[orders:]
    where = jnp.where(iota((8, number), 0) == 0, block_ref[...], cycle_ref[...])
    spread = (iota((number, rows), 1) // shells == iota((number, rows), 0)).astype(jnp.bfloat16)
    where = jnp.dot(
        where.astype(jnp.float32).astype(jnp.bfloat16), spread, preferred_element_type=jnp.float32
    ).astype(jnp.int32)
    block = where[0:1]
    cycle = where[1:2] + lax.axis_index("lens") * n_sim
    phase = 2 * bpx * block + (cycle & 1)
    turn_c, turn_s = cos_sin((m_col * phase) & (2 * NPIX - 1), 2 * NPIX)
    real, imag = turn_c * cosine - turn_s * sine, -(turn_s * cosine + turn_c * sine)
    pick = shells * cycles
    line, lane = iota((pick, rows), 0), iota((pick, rows), 1)
    chosen = (line == (lane % shells) * cycles + cycle).astype(jnp.bfloat16)
    r_high, r_low = split(real)
    i_high, i_low = split(imag)
    stacked = jnp.concatenate([r_high, i_high, r_low, i_low], axis=0)
    summed = lax.dot_general(stacked, chosen, NT, preferred_element_type=jnp.float32)
    summed = summed[: 2 * orders] + summed[2 * orders :]
    out_ref[...] = jnp.concatenate([summed[:orders], summed[orders:]], axis=1)


def fourier_terms(patches, patch_cycle, patch_block, m_values):
    number, shells, bpx = patches.shape
    orders = m_values.shape[0]
    cycles = lax.axis_size("sim") * lax.axis_size("lens")
    return pl.pallas_call(
        terms_kernel,
        out_shape=jax.ShapeDtypeStruct((orders, 2 * shells * cycles), jnp.float32),
        compiler_params=pltpu.CompilerParams(vmem_limit_bytes=48 << 20),
        name="fourier_terms",
    )(m_values.reshape(1, -1), patch_cycle.reshape(1, -1), patch_block.reshape(1, -1), patches)


def gram_kernel(own_ref, spin_ref, *refs):
    other_refs, out_ref = refs[:-1], refs[-1]
    m_dev, rows, lmax = own_ref.shape
    n_lens = lax.axis_size("lens")
    rank = lax.axis_index("lens")
    ell = iota((8, lmax), 1).astype(jnp.float32)
    factor = jnp.where(
        ell >= 2.0, jnp.sqrt((ell + 2.0) * (ell - 1.0) / jnp.maximum(ell * (ell + 1.0), 1.0)), 0.0
    )[0:1]
    for slot in range(m_dev):
        shear = (spin_ref[slot].astype(jnp.float32) * factor).astype(jnp.bfloat16)
        left = jnp.concatenate([own_ref[slot], shear], axis=0)
        right = jnp.concatenate([own_ref[slot]] + [r[slot] for r in other_refs], axis=0)
        gram = lax.dot_general(left, right, NT, preferred_element_type=jnp.float32)
        columns = []
        for column in range(n_lens):
            value = gram[:, :rows]
            for step in range(1, n_lens):
                value = jnp.where(
                    rank ^ step == column, gram[:, step * rows : (step + 1) * rows], value
                )
            columns.append(value)
        out_ref[slot] = jnp.concatenate(columns, axis=1)


def gram_matrices(own, spin, others):
    m_dev, rows, lmax = own.shape
    cycles = rows * lax.axis_size("lens")
    read = 2 * own.size * (2 + len(others))
    return pl.pallas_call(
        gram_kernel,
        out_shape=jax.ShapeDtypeStruct((m_dev, 2 * rows, cycles), jnp.float32),
        compiler_params=pltpu.CompilerParams(vmem_limit_bytes=48 << 20),
        cost_estimate=pl.CostEstimate(
            flops=4 * m_dev * rows * cycles * lmax, bytes_accessed=read, transcendentals=0
        ),
        name="gram_matrices",
    )(own, spin, *others)


def output_kernel(scale, weight_ref, modes_ref, gram_ref, kappa_ref, shear_ref):
    m_dev, _, cycles = gram_ref.shape
    rows = kappa_ref.shape[2]
    shells = weight_ref.shape[0]
    for slot in range(m_dev):
        modes = modes_ref[slot : slot + 1]
        parts = []
        for part in range(2):
            value = jnp.zeros((1, cycles), jnp.float32)
            for shell in range(shells):
                at = (part * shells + shell) * cycles
                value += modes[:, at : at + cycles] * (weight_ref[shell] * scale)
            parts.append(value)
        both = lax.dot_general(
            jnp.concatenate(parts, axis=0),
            gram_ref[slot],
            NT,
            precision=lax.Precision.HIGHEST,
            preferred_element_type=jnp.float32,
        )
        kappa_ref[slot] = both[:, :rows]
        shear_ref[slot] = both[:, rows:]


def outputs(weight, modes, gram, rows, scale):
    m_dev = gram.shape[0]
    shape = jax.ShapeDtypeStruct((m_dev, 2, rows), jnp.float32)
    vmem = pl.BlockSpec(memory_space=pltpu.VMEM)
    return pl.pallas_call(
        lambda *refs: output_kernel(scale, *refs),
        out_shape=(shape, shape),
        in_specs=[pl.BlockSpec(memory_space=pltpu.SMEM), vmem, vmem],
        out_specs=(vmem, vmem),
        compiler_params=pltpu.CompilerParams(vmem_limit_bytes=48 << 20),
        name="outputs",
    )(weight, modes, gram)


def on_device(
    patches, patch_cycle, patch_block, m_values, shell_weight, legendre_panel, spin2_panel
):
    n_sim = lax.axis_size("sim")
    n_lens = lax.axis_size("lens")
    m_dev, rows, lmax = legendre_panel.shape

    def swap(x, mask):
        pairs = [(i, i ^ mask) for i in range(n_sim * n_lens)]
        return lax.ppermute(x, ("sim", "lens"), pairs)

    others = [swap(legendre_panel, step) for step in range(1, n_lens)]
    terms = fourier_terms(patches, patch_cycle, patch_block, m_values)
    step = 1
    while step < n_lens:
        terms = terms + swap(terms, step)
        step *= 2
    gram = gram_matrices(legendre_panel, spin2_panel, others)
    half = n_sim // 2
    while half >= 1:
        kept = half * m_dev
        terms = terms[:kept] + swap(terms[kept:], half * n_lens + (1 if n_lens > 1 else 0))
        half //= 2
    scale = 1.0 / math.sqrt(NPIX * n_sim * n_lens * lmax)
    return outputs(shell_weight, terms, gram, rows, scale)


def solution(mesh):
    placed = (
        P(("sim", "lens"), None, None),
        P(("sim", "lens"), None),
        P(("sim", "lens")),
        P(),
        P(),
        P("sim", "lens", None),
        P("sim", "lens", None),
    )
    return jax.shard_map(
        on_device,
        mesh=mesh,
        in_specs=placed,
        out_specs=(P("sim", None, "lens"), P("sim", None, "lens")),
        check_vma=False,
    )
```

time: 121 us -> 21.5 us (0.18)
  blocking collectives: 78.7 us -> 0 us
  between operations: 14.8 us -> 0.7 us
  starting transfers between devices: 0.04 us -> 9.21 us
  waiting for transfers between devices: 13.7 us -> 6.25 us
  matrix products: 4.13 us -> 0 us
  local copies, waits for them, and re-layouts: 6.02 us -> 1.99 us
  other arithmetic: 3.37 us -> 0.02 us
  Pallas kernels: 0 us -> 3.15 us
    unnamed x1 -> x0, blocking collectives: 78.7 us -> none
    psum x1 -> x0, waiting for transfers between devices: 13.7 us -> none  [on_device(): lax.psum(partial_kappa.astype(jnp.bfloat16), 'lens').astype(jnp.float32)]
    ppermute x0 -> x6, starting transfers between devices: none -> 9.21 us  [swap(): return lax.ppermute(x, ('sim', 'lens'), pairs)]
    ppermute x0 -> x6, waiting for transfers between devices: none -> 6.25 us  [swap(): return lax.ppermute(x, ('sim', 'lens'), pairs)]
    dot_general x5 -> x0, matrix products: 4.13 us -> none  [the longest x1 1.79 us: on_device(): jnp.einsum('jcl,jrl->jcr', kappa_rounded, legendre_panel, preferred_eleme...]
    pallas_call x0 -> x3, Pallas kernels: none -> 3.15 us  [the longest x1 1.49 us: outputs(): pl.pallas_call(lambda *refs: output_kernel(scale, *refs), out_shape=(shap...]
    convert_element_type x1 -> x0, other arithmetic: 2.06 us -> none  [on_device(): partial_kappa.astype(jnp.bfloat16)]
    reshape x3 -> x0, local copies, waits for them, and re-layouts: 1.87 us -> none  [the longest x1 1.47 us: fourier_rows(): flat = rows.astype(jnp.float32).reshape(number * SHELLS, BPX)]
  transfers between devices with their start and end apart: 1 -> 6, of which waited for: 1 -> 5; matrix products, arithmetic and copies ran while one was open for 0% -> 0% of each run, Pallas kernels for 0% -> 0%
where the time goes in v1:
time: 21.5 us; the launch traced here: 21.3 us
  starting transfers between devices  9.21 us (43%)
  waiting for transfers between devices  6.25 us (29%)
  Pallas kernels  3.15 us (15%)
  local copies, waits for them, and re-layouts  1.99 us (9%)
  between operations  0.7 us (3%)
    ppermute x6, starting transfers between devices, swap(): return lax.ppermute(x, ('sim', 'lens'), pairs)  9.21 us
    ppermute x6, waiting for transfers between devices, swap(): return lax.ppermute(x, ('sim', 'lens'), pairs)  6.25 us
    unnamed x14, local copies, waits for them, and re-layouts  1.97 us
    pallas_call x1, Pallas kernels, outputs(): pl.pallas_call(lambda *refs: output_kernel(scale, *refs), out_shape=(shap...  1.49 us
    pallas_call x1, Pallas kernels, fourier_terms(): pl.pallas_call(terms_kernel, out_shape=jax.ShapeDtypeStruct((orders, 2 *...  1.1 us
    pallas_call x1, Pallas kernels, gram_matrices(): pl.pallas_call(gram_kernel, out_shape=jax.ShapeDtypeStruct((m_dev, 2 * ro...  0.56 us
  transfers between devices with their start and end apart: 6, of which 5 were waited for; matrix products, arithmetic and copies ran while one was open for 0% of the time, Pallas kernels for 0%

profile of v1, /device:TPU:0, one launch (start us, length us, event | category | flops | bytes accessed | tf_op | source)
XLA Modules:
  0.0 21.3 jit_solution(16429633015689938337)
XLA Ops:
  0.6 0.0 copy-start.3
  0.6 0.0 copy-start.4
  0.7 0.0 copy-start.5
  0.7 0.6 %copy-done.3 = s32[32]{0:T(128)S(1)} copy-done((s32[32]{0:T(128)S(1)}, s32[32]{0:T(128)}, u32[]{:S(2)}) %copy-start.3) | copy-done | bytes 152
  1.3 0.0 copy-done.4
  1.3 0.0 copy-done.5
  1.3 0.0 copy-start
  1.3 1.2 %copy-done = bf16[128,2,2048]{2,1,0:T(2,128)(2,1)S(1)} copy-done((bf16[128,2,2048]{2,1,0:T(2,128)(2,1)S(1)}, bf16[128,2,2048]{2,1,0:T(2,128)(2,1)}, u32[]{:S(2)}) %copy-start) | copy-done | bytes 1048600
  2.5 0.0 copy-start.1
  2.5 0.0 copy-start.2
  2.5 1.1 %fourier_terms.1 = f32[32,128]{1,0:T(8,128)S(1)} custom-call(s32[1,32]{1,0:T(1,128)S(1)} %bitcast.3, s32[1,128]{1,0:T(1,128)S(1)} %bitcast.4, s32[1,128]{1,0:T(1,128)S(1)} %bitcast.5, bf16[128,2,2048]{2,1,0:T(2,128)(2,1)S(1)} %copy-done), custom_call_target="tpu_custom_call" | custom-call | tf_op jit(solution)/shard_map/fourier_terms/pallas_call | solution.py:91
  3.7 0.5 %collective-permute-start = (f32[32,128]{1,0:T(8,128)S(1)}, f32[32,128]{1,0:T(8,128)S(1)}, u32[]{:S(2)}, u32[]{:S(2)}) collective-permute-start(f32[32,128]{1,0:T(8,128)S(1)} %fourier_terms.1), channel_id=1, source_target_pairs={{0,1},{1,0},{2,3},{3,2},{4,5},{5,4},{6,7},{7,6},{8,9},{9,8},{10,11... | collective-permute-start | bytes 49160 | tf_op jit(solution)/shard_map/ppermute | solution.py:186
  4.2 0.8 %collective-permute-done = f32[32,128]{1,0:T(8,128)S(1)} collective-permute-done((f32[32,128]{1,0:T(8,128)S(1)}, f32[32,128]{1,0:T(8,128)S(1)}, u32[]{:S(2)}, u32[]{:S(2)}) %collective-permute-start) | collective-permute-done | bytes 16416 | tf_op jit(solution)/shard_map/ppermute | solution.py:186
  5.0 3.7 %collective-permute-start.1 = (f32[16,128]{1,0:T(8,128)S(1)}, f32[16,128]{1,0:T(8,128)S(1)}, u32[]{:S(2)}, u32[]{:S(2)}) collective-permute-start(f32[16,128]{1,0:T(8,128)S(1)} %slice.33), channel_id=1, source_target_pairs={{0,17},{1,16},{2,19},{3,18},{4,21},{5,20},{6,23},{7,22},{8,25},{9,... | collective-permute-start | bytes 24584 | tf_op jit(solution)/shard_map/ppermute | solution.py:186
  8.7 1.4 %collective-permute-done.1 = f32[16,128]{1,0:T(8,128)S(1)} collective-permute-done((f32[16,128]{1,0:T(8,128)S(1)}, f32[16,128]{1,0:T(8,128)S(1)}, u32[]{:S(2)}, u32[]{:S(2)}) %collective-permute-start.1) | collective-permute-done | bytes 8224 | tf_op jit(solution)/shard_map/ppermute | solution.py:186
  10.1 1.6 %collective-permute-start.2 = (f32[8,128]{1,0:T(8,128)S(1)}, f32[8,128]{1,0:T(8,128)S(1)}, u32[]{:S(2)}, u32[]{:S(2)}) collective-permute-start(f32[8,128]{1,0:T(8,128)S(1)} %slice.35), channel_id=1, source_target_pairs={{0,9},{1,8},{2,11},{3,10},{4,13},{5,12},{6,15},{7,14},{8,1},{9,0},... | collective-permute-start | bytes 12296 | tf_op jit(solution)/shard_map/ppermute | solution.py:186
  11.7 0.0 copy-done.1
  11.7 0.3 %collective-permute-start.5 = (bf16[2,16,8192]{2,1,0:T(8,128)(2,1)S(1)}, bf16[2,16,8192]{2,1,0:T(8,128)(2,1)S(1)}, u32[]{:S(2)}, u32[]{:S(2)}) collective-permute-start(bf16[2,16,8192]{2,1,0:T(8,128)(2,1)S(1)} %copy-done.1), channel_id=1, source_target_pairs={{0,1},{1,0},{2,3},{3,2},{4,5},{5,4},{6,7},{7,6},{8,9},{9,8},{10,11... | collective-permute-start | bytes 1572872 | tf_op jit(solution)/shard_map/ppermute | solution.py:186
  12.0 1.1 %collective-permute-done.2 = f32[8,128]{1,0:T(8,128)S(1)} collective-permute-done((f32[8,128]{1,0:T(8,128)S(1)}, f32[8,128]{1,0:T(8,128)S(1)}, u32[]{:S(2)}, u32[]{:S(2)}) %collective-permute-start.2) | collective-permute-done | bytes 4128 | tf_op jit(solution)/shard_map/ppermute | solution.py:186
  13.1 1.5 %collective-permute-start.3 = (f32[4,128]{1,0:T(4,128)S(1)}, f32[4,128]{1,0:T(4,128)S(1)}, u32[]{:S(2)}, u32[]{:S(2)}) collective-permute-start(f32[4,128]{1,0:T(4,128)S(1)} %slice.29), channel_id=1, source_target_pairs={{0,5},{1,4},{2,7},{3,6},{4,1},{5,0},{6,3},{7,2},{8,13},{9,12},{10,... | collective-permute-start | bytes 6152 | tf_op jit(solution)/shard_map/ppermute | solution.py:186
  14.7 1.5 %collective-permute-done.3 = f32[4,128]{1,0:T(4,128)S(1)} collective-permute-done((f32[4,128]{1,0:T(4,128)S(1)}, f32[4,128]{1,0:T(4,128)S(1)}, u32[]{:S(2)}, u32[]{:S(2)}) %collective-permute-start.3) | collective-permute-done | bytes 2080 | tf_op jit(solution)/shard_map/ppermute | solution.py:186
  16.2 1.5 %collective-permute-start.4 = (f32[2,128]{1,0:T(2,128)S(1)}, f32[2,128]{1,0:T(2,128)S(1)}, u32[]{:S(2)}, u32[]{:S(2)}) collective-permute-start(f32[2,128]{1,0:T(2,128)S(1)} %slice.31), channel_id=1, source_target_pairs={{0,3},{1,2},{2,1},{3,0},{4,7},{5,6},{6,5},{7,4},{8,11},{9,10},{10,... | collective-permute-start | bytes 3080 | tf_op jit(solution)/shard_map/ppermute | solution.py:186
  17.7 1.5 %collective-permute-done.4 = f32[2,128]{1,0:T(2,128)S(1)} collective-permute-done((f32[2,128]{1,0:T(2,128)S(1)}, f32[2,128]{1,0:T(2,128)S(1)}, u32[]{:S(2)}, u32[]{:S(2)}) %collective-permute-start.4) | collective-permute-done | bytes 1056 | tf_op jit(solution)/shard_map/ppermute | solution.py:186
  19.2 0.0 copy-start.6
  19.2 0.0 collective-permute-done.5.refs_0_
  19.2 0.0 copy-done.2
  19.2 0.6 %gram_matrices.1.refs_2_ = f32[2,32,32]{2,1,0:T(8,128)S(1)} custom-call(bf16[2,16,8192]{2,1,0:T(8,128)(2,1)S(1)} %copy-done.1, bf16[2,16,8192]{2,1,0:T(8,128)(2,1)S(1)} %copy-done.2, bf16[2,16,8192]{2,1,0:T(8,128)(2,1)S(1)} %collective-permute-done.5.refs_0_), custom_call_target="tpu_custom_call" | custom-call | flops 33554432 | bytes 1572864 | tf_op jit(solution)/shard_map/gram_matrices/pallas_call | solution.py:128
  19.7 0.1 copy-done.6
  19.8 1.5 %outputs.1 = (f32[2,2,16]{2,1,0:T(2,128)}, f32[2,2,16]{2,1,0:T(2,128)}) custom-call(f32[2]{0:T(128)S(1)} %copy-done.6, f32[2,128]{1,0:T(2,128)S(1)} %slice_add_fusion.3.refs_1_, f32[2,32,32]{2,1,0:T(8,128)S(1)} %gram_matrices.1.refs_2_), custom_call_target="tpu_custom_call" | custom-call | tf_op jit(solution)/shard_map/outputs/pallas_call | solution.py:167
  (9 shorter events, 0.0 us)
Async XLA Ops:
  0.6 0.7 %copy-start.3 = (s32[32]{0:T(128)S(1)}, s32[32]{0:T(128)}, u32[]{:S(2)}) copy-start(s32[32]{0:T(128)} %param.10) | copy-start | bytes 388
  0.6 0.7 %copy-start.4 = (s32[128,1]{0,1:T(1,128)S(1)}, s32[128,1]{0,1:T(1,128)}, u32[]{:S(2)}) copy-start(s32[128,1]{0,1:T(1,128)} %param.8) | copy-start | bytes 1540
  0.7 0.7 %copy-start.5 = (s32[128]{0:T(128)S(1)}, s32[128]{0:T(128)}, u32[]{:S(2)}) copy-start(s32[128]{0:T(128)} %param.9) | copy-start | bytes 1540
  1.3 1.2 %copy-start = (bf16[128,2,2048]{2,1,0:T(2,128)(2,1)S(1)}, bf16[128,2,2048]{2,1,0:T(2,128)(2,1)}, u32[]{:S(2)}) copy-start(bf16[128,2,2048]{2,1,0:T(2,128)(2,1)} %patch_ref.1) | copy-start | bytes 3145732
  2.5 9.1 %copy-start.1 = (bf16[2,16,8192]{2,1,0:T(8,128)(2,1)S(1)}, bf16[2,16,8192]{2,1,0:T(8,128)(2,1)}, u32[]{:S(2)}) copy-start(bf16[2,16,8192]{2,1,0:T(8,128)(2,1)} %own_ref.1) | copy-start | bytes 1572868
  2.5 16.6 %copy-start.2 = (bf16[2,16,8192]{2,1,0:T(8,128)(2,1)S(1)}, bf16[2,16,8192]{2,1,0:T(8,128)(2,1)}, u32[]{:S(2)}) copy-start(bf16[2,16,8192]{2,1,0:T(8,128)(2,1)} %spin_ref.1) | copy-start | bytes 1572868
  3.7 1.4 %collective-permute-start = (f32[32,128]{1,0:T(8,128)S(1)}, f32[32,128]{1,0:T(8,128)S(1)}, u32[]{:S(2)}, u32[]{:S(2)}) collective-permute-start(f32[32,128]{1,0:T(8,128)S(1)} %fourier_terms.1), channel_id=1, source_target_pairs={{0,1},{1,0},{2,3},{3,2},{4,5},{5,4},{6,7},{7,6},{8,9},{9,8},{10,11... | collective-permute-start | bytes 49160 | tf_op jit(solution)/shard_map/ppermute | solution.py:186
  5.0 5.1 %collective-permute-start.1 = (f32[16,128]{1,0:T(8,128)S(1)}, f32[16,128]{1,0:T(8,128)S(1)}, u32[]{:S(2)}, u32[]{:S(2)}) collective-permute-start(f32[16,128]{1,0:T(8,128)S(1)} %slice.33), channel_id=1, source_target_pairs={{0,17},{1,16},{2,19},{3,18},{4,21},{5,20},{6,23},{7,22},{8,25},{9,... | collective-permute-start | bytes 24584 | tf_op jit(solution)/shard_map/ppermute | solution.py:186
  10.1 3.0 %collective-permute-start.2 = (f32[8,128]{1,0:T(8,128)S(1)}, f32[8,128]{1,0:T(8,128)S(1)}, u32[]{:S(2)}, u32[]{:S(2)}) collective-permute-start(f32[8,128]{1,0:T(8,128)S(1)} %slice.35), channel_id=1, source_target_pairs={{0,9},{1,8},{2,11},{3,10},{4,13},{5,12},{6,15},{7,14},{8,1},{9,0},... | collective-permute-start | bytes 12296 | tf_op jit(solution)/shard_map/ppermute | solution.py:186
  11.7 7.5 %collective-permute-start.5 = (bf16[2,16,8192]{2,1,0:T(8,128)(2,1)S(1)}, bf16[2,16,8192]{2,1,0:T(8,128)(2,1)S(1)}, u32[]{:S(2)}, u32[]{:S(2)}) collective-permute-start(bf16[2,16,8192]{2,1,0:T(8,128)(2,1)S(1)} %copy-done.1), channel_id=1, source_target_pairs={{0,1},{1,0},{2,3},{3,2},{4,5},{5,4},{6,7},{7,6},{8,9},{9,8},{10,11... | collective-permute-start | bytes 1572872 | tf_op jit(solution)/shard_map/ppermute | solution.py:186
  13.1 3.0 %collective-permute-start.3 = (f32[4,128]{1,0:T(4,128)S(1)}, f32[4,128]{1,0:T(4,128)S(1)}, u32[]{:S(2)}, u32[]{:S(2)}) collective-permute-start(f32[4,128]{1,0:T(4,128)S(1)} %slice.29), channel_id=1, source_target_pairs={{0,5},{1,4},{2,7},{3,6},{4,1},{5,0},{6,3},{7,2},{8,13},{9,12},{10,... | collective-permute-start | bytes 6152 | tf_op jit(solution)/shard_map/ppermute | solution.py:186
  16.2 3.0 %collective-permute-start.4 = (f32[2,128]{1,0:T(2,128)S(1)}, f32[2,128]{1,0:T(2,128)S(1)}, u32[]{:S(2)}, u32[]{:S(2)}) collective-permute-start(f32[2,128]{1,0:T(2,128)S(1)} %slice.31), channel_id=1, source_target_pairs={{0,3},{1,2},{2,1},{3,0},{4,7},{5,6},{6,5},{7,4},{8,11},{9,10},{10,... | collective-permute-start | bytes 3080 | tf_op jit(solution)/shard_map/ppermute | solution.py:186
  19.2 0.7 %copy-start.6 = (f32[2]{0:T(128)S(1)}, f32[2]{0:T(128)}, u32[]{:S(2)}) copy-start(f32[2]{0:T(128)} %refs_0_.1) | copy-start | bytes 28

commit v2 on v1

v2 whole, which is shorter than its diff:
```python
import math

import jax
import jax.numpy as jnp
from jax import lax
from jax.experimental import pallas as pl
from jax.experimental.pallas import tpu as pltpu
from jax.sharding import PartitionSpec as P

NPIX = 16384
NT = (((1,), (1,)), ((), ()))
PIECES = 1


def cos_sin(index, turn):
    quarter = turn // 4
    quadrant = (index + quarter // 2) // quarter
    r = (index - quadrant * quarter).astype(jnp.float32) * (2.0 * math.pi / turn)
    q = r * r
    sine = r + r * q * (-1.0 / 6 + q * (1.0 / 120 + q * (-1.0 / 5040 + q * (1.0 / 362880))))
    cosine = 1.0 + q * (-0.5 + q * (1.0 / 24 + q * (-1.0 / 720 + q * (1.0 / 40320))))
    odd = (quadrant & 1) == 1
    c = jnp.where(odd, sine, cosine)
    s = jnp.where(odd, cosine, sine)
    c = jnp.where(((quadrant + 1) & 2) == 2, -c, c)
    s = jnp.where((quadrant & 2) == 2, -s, s)
    return c, s


def split(x):
    high = x.astype(jnp.bfloat16)
    return high, (x - high.astype(jnp.float32)).astype(jnp.bfloat16)


def iota(shape, dim):
    return lax.broadcasted_iota(jnp.int32, shape, dim)


def terms_kernel(
    scale, m_hbm, cycle_hbm, block_hbm, weight_hbm, patch_hbm, out_ref,
    m_ref, cycle_ref, block_ref, weight_ref, patch_ref, table_ref, small_sem, patch_sem
):
    number, shells, bpx = patch_ref.shape
    orders = m_ref.shape[1]
    n_sim = lax.axis_size("sim")
    m_dev = orders // n_sim
    small = [
        pltpu.make_async_copy(source, target, small_sem.at[i])
        for i, (source, target) in enumerate(
            ((m_hbm, m_ref), (cycle_hbm, cycle_ref), (block_hbm, block_ref), (weight_hbm, weight_ref))
        )
    ]
    width = bpx // PIECES
    large = [
        pltpu.make_async_copy(
            patch_hbm.at[:, :, pl.ds(i * width, width)],
            patch_ref.at[:, :, pl.ds(i * width, width)],
            patch_sem.at[i],
        )
        for i in range(PIECES)
    ]
    for copy in small + large:
        copy.start()
    square = (orders, orders)
    row = iota(square, 0)
    slot = (row % n_sim) * m_dev + row // n_sim
    for copy in small:
        copy.wait()
    m_row = m_ref[...].astype(jnp.float32)
    m_col = jnp.sum(jnp.where(slot == iota(square, 1), m_row, 0.0), axis=1, keepdims=True)
    m_col = m_col.astype(jnp.int32)
    low_c, low_s = cos_sin((m_col * iota((orders, 128), 1)) & (NPIX - 1), NPIX)
    parts = bpx // 128
    high_c, high_s = cos_sin((m_col * (128 * iota((orders, 128), 1))) & (NPIX - 1), NPIX)
    rows = number * shells
    where = jnp.where(iota((8, number), 0) == 0, block_ref[...], cycle_ref[...])
    spread = (iota((number, rows), 1) // shells == iota((number, rows), 0)).astype(jnp.bfloat16)
    where = jnp.dot(
        where.astype(jnp.float32).astype(jnp.bfloat16), spread, preferred_element_type=jnp.float32
    ).astype(jnp.int32)
    block, cycle = where[0:1], where[1:2]
    parity = (cycle + lax.axis_index("lens") * n_sim) & 1
    phase = 2 * bpx * block + parity
    turn_c, turn_s = cos_sin((m_col * phase) & (2 * NPIX - 1), 2 * NPIX)
    lane = iota((1, rows), 1) % shells
    weight = jnp.zeros((1, rows), jnp.float32)
    for shell in range(shells):
        weight = jnp.where(lane == shell, weight_ref[0:1, shell : shell + 1] * scale, weight)
    turn_c, turn_s = turn_c * weight, turn_s * weight
    chosen = (iota((n_sim, rows), 0) == cycle).astype(jnp.bfloat16)
    for part in range(parts):
        hc = high_c[:, part : part + 1]
        hs = high_s[:, part : part + 1]
        c_high, c_low = split(low_c * hc - low_s * hs)
        s_high, s_low = split(low_s * hc + low_c * hs)
        table_ref[:, part * 128 : (part + 1) * 128] = jnp.concatenate(
            [c_high, s_high, c_low, s_low], axis=0
        )
    total = jnp.zeros((4 * orders, rows), jnp.float32)
    for piece, copy in enumerate(large):
        copy.wait()
        at = slice(piece * width, (piece + 1) * width)
        total += lax.dot_general(
            table_ref[:, at],
            patch_ref[:, :, at].reshape(rows, width),
            NT,
            preferred_element_type=jnp.float32,
        )
    total = total[: 2 * orders] + total[2 * orders :]
    cosine, sine = total[:orders], total[orders:]
    real, imag = turn_c * cosine - turn_s * sine, -(turn_s * cosine + turn_c * sine)
    r_high, r_low = split(real)
    i_high, i_low = split(imag)
    stacked = jnp.concatenate([r_high, i_high, r_low, i_low], axis=0)
    summed = lax.dot_general(stacked, chosen, NT, preferred_element_type=jnp.float32)
    summed = summed[: 2 * orders] + summed[2 * orders :]
    real, imag = summed[:orders], summed[orders:]
    pieces = []
    for slot in range(m_dev):
        at = slice(slot * n_sim, (slot + 1) * n_sim)
        pieces += [real[at], imag[at]]
    value = jnp.concatenate(pieces, axis=1)
    for column in range(lax.axis_size("lens")):
        out_ref[:, column] = value


def fourier_terms(patches, patch_cycle, patch_block, m_values, shell_weight, scale):
    number, shells, bpx = patches.shape
    orders = m_values.shape[0]
    n_sim, n_lens = lax.axis_size("sim"), lax.axis_size("lens")
    small = [
        m_values.reshape(1, -1),
        patch_cycle.reshape(1, -1),
        patch_block.reshape(1, -1),
        shell_weight.reshape(1, -1),
    ]
    width = orders // n_sim * 2 * n_sim
    return pl.pallas_call(
        lambda *refs: terms_kernel(scale, *refs),
        out_shape=jax.ShapeDtypeStruct((n_sim, n_lens, width), jnp.float32),
        in_specs=[pl.BlockSpec(memory_space=pltpu.HBM)] * 5,
        out_specs=pl.BlockSpec(memory_space=pltpu.VMEM),
        scratch_shapes=[pltpu.VMEM(x.shape, x.dtype) for x in small]
        + [
            pltpu.VMEM(patches.shape, patches.dtype),
            pltpu.VMEM((4 * orders, bpx), jnp.bfloat16),
            pltpu.SemaphoreType.DMA((4,)),
            pltpu.SemaphoreType.DMA((PIECES,)),
        ],
        compiler_params=pltpu.CompilerParams(vmem_limit_bytes=48 << 20),
        name="fourier_terms",
    )(*[pltpu.with_memory_space_constraint(x, pltpu.HBM) for x in small + [patches]])


def finish_kernel(terms_ref, own_ref, spin_ref, *refs):
    other_refs, (kappa_ref, shear_ref) = refs[:-2], refs[-2:]
    m_dev, rows, lmax = own_ref.shape
    n_lens = lax.axis_size("lens")
    rank = lax.axis_index("lens")
    ell = iota((8, lmax), 1).astype(jnp.float32)
    factor = jnp.where(
        ell >= 2.0, jnp.sqrt((ell + 2.0) * (ell - 1.0) / jnp.maximum(ell * (ell + 1.0), 1.0)), 0.0
    )[0:1]
    steps = range(n_lens)
    modes = [jnp.sum(terms_ref[:, rank ^ step], axis=0, keepdims=True) for step in steps]
    same = iota((rows, rows), 0) == iota((rows, rows), 1)
    for slot in range(m_dev):
        columns = []
        for part in range(2):
            at = (slot * 2 + part) * rows
            columns.append(
                jnp.concatenate(
                    [
                        jnp.sum(jnp.where(same, m[:, at : at + rows], 0.0), axis=1, keepdims=True)
                        for m in modes
                    ],
                    axis=0,
                )
            )
        shear = (spin_ref[slot].astype(jnp.float32) * factor).astype(jnp.bfloat16)
        left = jnp.concatenate([own_ref[slot], shear], axis=0)
        right = jnp.concatenate([own_ref[slot]] + [r[slot] for r in other_refs], axis=0)
        gram = lax.dot_general(right, left, NT, preferred_element_type=jnp.float32)
        for part in range(2):
            both = jnp.sum(gram * columns[part], axis=0, keepdims=True)
            kappa_ref[slot, part : part + 1] = both[:, :rows]
            shear_ref[slot, part : part + 1] = both[:, rows:]


def finish(terms, own, spin, others):
    m_dev, rows, lmax = own.shape
    shape = jax.ShapeDtypeStruct((m_dev, 2, rows), jnp.float32)
    cycles = rows * (1 + len(others))
    return pl.pallas_call(
        finish_kernel,
        out_shape=(shape, shape),
        compiler_params=pltpu.CompilerParams(vmem_limit_bytes=48 << 20),
        cost_estimate=pl.CostEstimate(
            flops=4 * m_dev * rows * cycles * lmax,
            bytes_accessed=2 * own.size * (2 + len(others)),
            transcendentals=0,
        ),
        name="finish",
    )(terms, own, spin, *others)


def on_device(
    patches, patch_cycle, patch_block, m_values, shell_weight, legendre_panel, spin2_panel
):
    n_sim = lax.axis_size("sim")
    n_lens = lax.axis_size("lens")
    m_dev, rows, lmax = legendre_panel.shape
    axes = ("sim", "lens")

    def swap(x, mask):
        return lax.ppermute(x, axes, [(i, i ^ mask) for i in range(n_sim * n_lens)])

    others = [swap(legendre_panel, step) for step in range(1, n_lens)]
    scale = 1.0 / math.sqrt(NPIX * n_sim * n_lens * lmax)
    terms = fourier_terms(patches, patch_cycle, patch_block, m_values, shell_weight, scale)
    terms = terms.reshape(n_sim * n_lens, 1, -1)
    terms = lax.all_to_all(terms, axes, 0, 0, tiled=True)
    return finish(terms.reshape(n_sim, n_lens, -1), legendre_panel, spin2_panel, others)


def solution(mesh):
    placed = (
        P(("sim", "lens"), None, None),
        P(("sim", "lens"), None),
        P(("sim", "lens")),
        P(),
        P(),
        P("sim", "lens", None),
        P("sim", "lens", None),
    )
    return jax.shard_map(
        on_device,
        mesh=mesh,
        in_specs=placed,
        out_specs=(P("sim", None, "lens"), P("sim", None, "lens")),
        check_vma=False,
    )
```

time: 21.5 us -> 18.6 us (0.87)
  blocking collectives: 0 us -> 13.9 us
  starting transfers between devices: 9.21 us -> 0.52 us
  waiting for transfers between devices: 6.25 us -> 0.01 us
  local copies, waits for them, and re-layouts: 1.99 us -> 0.01 us
    all_to_all x0 -> x1, blocking collectives: none -> 13.9 us  [on_device(): terms = lax.all_to_all(terms, axes, 0, 0, tiled=True)]
    ppermute x6 -> x1, starting transfers between devices: 9.21 us -> 0.52 us  [swap(): return lax.ppermute(x, axes, [(i, i ^ mask) for i in range(n_sim * n_lens)])]
    ppermute x6 -> x1, waiting for transfers between devices: 6.25 us -> 0.01 us  [swap(): return lax.ppermute(x, axes, [(i, i ^ mask) for i in range(n_sim * n_lens)])]
    unnamed x14 -> x4, local copies, waits for them, and re-layouts: 1.97 us -> 0.01 us
    pallas_call x3 -> x2, Pallas kernels: 3.15 us -> 3.3 us  [the longest x1 2.18 us: fourier_terms(): pl.pallas_call(lambda *refs: terms_kernel(scale, *refs), out_shape=jax.Sh...]
  transfers between devices with their start and end apart: 6 -> 1, of which waited for: 5 -> 0; matrix products, arithmetic and copies ran while one was open for 0% -> 0% of each run, Pallas kernels for 0% -> 12%
where the time goes in v2:
time: 18.6 us; the launch traced here: 18.4 us
  blocking collectives  13.9 us (75%)
  Pallas kernels  3.3 us (18%)
  between operations  0.65 us (3%)
  starting transfers between devices  0.52 us (3%)
    all_to_all x1, blocking collectives, on_device(): terms = lax.all_to_all(terms, axes, 0, 0, tiled=True)  13.9 us
    pallas_call x1, Pallas kernels, fourier_terms(): pl.pallas_call(lambda *refs: terms_kernel(scale, *refs), out_shape=jax.Sh...  2.18 us
    pallas_call x1, Pallas kernels, finish(): pl.pallas_call(finish_kernel, out_shape=(shape, shape), compiler_params=p...  1.12 us
    ppermute x1, starting transfers between devices, swap(): return lax.ppermute(x, axes, [(i, i ^ mask) for i in range(n_sim * n_lens)])  0.52 us
  transfers between devices with their start and end apart: 1, of which 0 were waited for; matrix products, arithmetic and copies ran while one was open for 0% of the time, Pallas kernels for 12%

profile of v2, /device:TPU:0, one launch (start us, length us, event | category | flops | bytes accessed | tf_op | source)
XLA Modules:
  0.0 18.4 jit_solution(18323450815574118349)
XLA Ops:
  0.6 0.5 %collective-permute-start = (bf16[2,16,8192]{2,1,0:T(8,128)(2,1)}, bf16[2,16,8192]{2,1,0:T(8,128)(2,1)S(1)}, u32[]{:S(2)}, u32[]{:S(2)}) collective-permute-start(bf16[2,16,8192]{2,1,0:T(8,128)(2,1)} %own_ref.1), channel_id=1, source_target_pairs={{0,1},{1,0},{2,3},{3,2},{4,5},{5,4},{6,7},{7,6},{8,9},{9,8},{10,11... | collective-permute-start | bytes 1572872 | tf_op jit(solution)/shard_map/ppermute | solution.py:216
  1.2 0.0 copy-start
  1.2 0.0 copy-start.1
  1.2 2.2 %fourier_terms.1 = f32[16,2,64]{2,1,0:T(2,128)S(1)} custom-call(s32[1,32]{1,0:T(1,128)} %bitcast.10, s32[1,128]{1,0:T(1,128)} %bitcast.11, s32[1,128]{1,0:T(1,128)} %bitcast.12, f32[1,2]{1,0:T(1,128)} %bitcast.13, bf16[128,2,2048]{2,1,0:T(2,128)(2,1)} %refs_4_.1), custom_call_target="tpu_custom_call" | custom-call | tf_op jit(solution)/shard_map/fourier_terms/pallas_call | solution.py:138
  3.3 13.9 %all_to_all.5 = f32[32,1,64]{2,1,0:T(1,128)S(1)} all-to-all(f32[32,1,64]{2,1,0:T(1,128)S(1)} %bitcast.9), channel_id=1, replica_groups=mesh['sim'=16,'lens'=2] {'sim','lens'}, dimensions={0} | all-to-all | bytes 16384 | tf_op jit(solution)/shard_map/all_to_all | solution.py:222
  17.3 0.0 collective-permute-done.refs_0_
  17.3 0.0 copy-done
  17.3 0.0 copy-done.1
  17.3 1.1 %finish.1 = (f32[2,2,16]{2,1,0:T(2,128)}, f32[2,2,16]{2,1,0:T(2,128)}) custom-call(f32[16,2,64]{2,1,0:T(2,128)S(1)} %bitcast.8, bf16[2,16,8192]{2,1,0:T(8,128)(2,1)S(1)} %copy-done, bf16[2,16,8192]{2,1,0:T(8,128)(2,1)S(1)} %copy-done.1, bf16[2,16,8192]{2,1,0:T(8,128)(2,1)S(1)} %collective-permute-done.refs_0_), custom_call_target="tpu_custom_call" | custom-call | flops 33554432 | bytes 1572864 | tf_op jit(solution)/shard_map/finish/pallas_call | solution.py:194
Async XLA Ops:
  0.6 16.6 %collective-permute-start = (bf16[2,16,8192]{2,1,0:T(8,128)(2,1)}, bf16[2,16,8192]{2,1,0:T(8,128)(2,1)S(1)}, u32[]{:S(2)}, u32[]{:S(2)}) collective-permute-start(bf16[2,16,8192]{2,1,0:T(8,128)(2,1)} %own_ref.1), channel_id=1, source_target_pairs={{0,1},{1,0},{2,3},{3,2},{4,5},{5,4},{6,7},{7,6},{8,9},{9,8},{10,11... | collective-permute-start | bytes 1572872 | tf_op jit(solution)/shard_map/ppermute | solution.py:216
  1.2 16.1 %copy-start = (bf16[2,16,8192]{2,1,0:T(8,128)(2,1)S(1)}, bf16[2,16,8192]{2,1,0:T(8,128)(2,1)}, u32[]{:S(2)}) copy-start(bf16[2,16,8192]{2,1,0:T(8,128)(2,1)} %own_ref.1) | copy-start | bytes 1572868
  1.2 16.1 %copy-start.1 = (bf16[2,16,8192]{2,1,0:T(8,128)(2,1)S(1)}, bf16[2,16,8192]{2,1,0:T(8,128)(2,1)}, u32[]{:S(2)}) copy-start(bf16[2,16,8192]{2,1,0:T(8,128)(2,1)} %spin_ref.1) | copy-start | bytes 1572868

commit v3 on v2

--- a/solution.py
+++ b/solution.py
@@ -10,6 +10,7 @@
 NPIX = 16384
 NT = (((1,), (1,)), ((), ()))
 PIECES = 1
+GROUP = 8
 
 
 def cos_sin(index, turn):
@@ -38,7 +39,7 @@
 
 def terms_kernel(
     scale, m_hbm, cycle_hbm, block_hbm, weight_hbm, patch_hbm, out_ref,
-    m_ref, cycle_ref, block_ref, weight_ref, patch_ref, table_ref, small_sem, patch_sem
+    m_ref, cycle_ref, block_ref, weight_ref, patch_ref, small_sem, patch_sem
 ):
     number, shells, bpx = patch_ref.shape
     orders = m_ref.shape[1]
@@ -88,23 +89,19 @@
         weight = jnp.where(lane == shell, weight_ref[0:1, shell : shell + 1] * scale, weight)
     turn_c, turn_s = turn_c * weight, turn_s * weight
     chosen = (iota((n_sim, rows), 0) == cycle).astype(jnp.bfloat16)
-    for part in range(parts):
-        hc = high_c[:, part : part + 1]
-        hs = high_s[:, part : part + 1]
-        c_high, c_low = split(low_c * hc - low_s * hs)
-        s_high, s_low = split(low_s * hc + low_c * hs)
-        table_ref[:, part * 128 : (part + 1) * 128] = jnp.concatenate(
-            [c_high, s_high, c_low, s_low], axis=0
-        )
+    large[0].wait()
     total = jnp.zeros((4 * orders, rows), jnp.float32)
-    for piece, copy in enumerate(large):
-        copy.wait()
-        at = slice(piece * width, (piece + 1) * width)
+    for first in range(0, parts, GROUP):
+        tables = []
+        for part in range(first, first + GROUP):
+            hc = high_c[:, part : part + 1]
+            hs = high_s[:, part : part + 1]
+            c_high, c_low = split(low_c * hc - low_s * hs)
+            s_high, s_low = split(low_s * hc + low_c * hs)
+            tables.append(jnp.concatenate([c_high, s_high, c_low, s_low], axis=0))
+        chunk = patch_ref[:, :, first * 128 : (first + GROUP) * 128].reshape(rows, GROUP * 128)
         total += lax.dot_general(
-            table_ref[:, at],
-            patch_ref[:, :, at].reshape(rows, width),
-            NT,
-            preferred_element_type=jnp.float32,
+            jnp.concatenate(tables, axis=1), chunk, NT, preferred_element_type=jnp.float32
         )
     total = total[: 2 * orders] + total[2 * orders :]
     cosine, sine = total[:orders], total[orders:]
@@ -143,7 +140,6 @@
         scratch_shapes=[pltpu.VMEM(x.shape, x.dtype) for x in small]
         + [
             pltpu.VMEM(patches.shape, patches.dtype),
-            pltpu.VMEM((4 * orders, bpx), jnp.bfloat16),
             pltpu.SemaphoreType.DMA((4,)),
             pltpu.SemaphoreType.DMA((PIECES,)),
         ],
@@ -159,7 +155,7 @@
     rank = lax.axis_index("lens")
     ell = iota((8, lmax), 1).astype(jnp.float32)
     factor = jnp.where(
-        ell >= 2.0, jnp.sqrt((ell + 2.0) * (ell - 1.0) / jnp.maximum(ell * (ell + 1.0), 1.0)), 0.0
+        ell >= 2.0, jnp.sqrt(1.0 - 2.0 / jnp.maximum(ell * (ell + 1.0), 2.0)), 0.0
     )[0:1]
     steps = range(n_lens)
     modes = [jnp.sum(terms_ref[:, rank ^ step], axis=0, keepdims=True) for step in steps]

time: 18.6 us -> 18.5 us (level)
  no operation moved by 1% of the time
where the time goes in v3:
time: 18.5 us; the launch traced here: 18.3 us
  blocking collectives  13.9 us (75%)
  Pallas kernels  3.24 us (18%)
  between operations  0.65 us (4%)
  starting transfers between devices  0.52 us (3%)
    all_to_all x1, blocking collectives, on_device(): terms = lax.all_to_all(terms, axes, 0, 0, tiled=True)  13.9 us
    pallas_call x1, Pallas kernels, fourier_terms(): pl.pallas_call(lambda *refs: terms_kernel(scale, *refs), out_shape=jax.Sh...  2.13 us
    pallas_call x1, Pallas kernels, finish(): pl.pallas_call(finish_kernel, out_shape=(shape, shape), compiler_params=p...  1.11 us
    ppermute x1, starting transfers between devices, swap(): return lax.ppermute(x, axes, [(i, i ^ mask) for i in range(n_sim * n_lens)])  0.52 us
  transfers between devices with their start and end apart: 1, of which 0 were waited for; matrix products, arithmetic and copies ran while one was open for 0% of the time, Pallas kernels for 12%

profile of v3, /device:TPU:0, one launch (start us, length us, event | category | flops | bytes accessed | tf_op | source)
XLA Modules:
  0.0 18.3 jit_solution(15993998702375343638)
XLA Ops:
  0.6 0.5 %collective-permute-start = (bf16[2,16,8192]{2,1,0:T(8,128)(2,1)}, bf16[2,16,8192]{2,1,0:T(8,128)(2,1)S(1)}, u32[]{:S(2)}, u32[]{:S(2)}) collective-permute-start(bf16[2,16,8192]{2,1,0:T(8,128)(2,1)} %own_ref.1), channel_id=1, source_target_pairs={{0,1},{1,0},{2,3},{3,2},{4,5},{5,4},{6,7},{7,6},{8,9},{9,8},{10,11... | collective-permute-start | bytes 1572872 | tf_op jit(solution)/shard_map/ppermute | solution.py:212
  1.2 0.0 copy-start
  1.2 0.0 copy-start.1
  1.2 2.1 %fourier_terms.1 = f32[16,2,64]{2,1,0:T(2,128)S(1)} custom-call(s32[1,32]{1,0:T(1,128)} %bitcast.10, s32[1,128]{1,0:T(1,128)} %bitcast.11, s32[1,128]{1,0:T(1,128)} %bitcast.12, f32[1,2]{1,0:T(1,128)} %bitcast.13, bf16[128,2,2048]{2,1,0:T(2,128)(2,1)} %refs_4_.1), custom_call_target="tpu_custom_call" | custom-call | tf_op jit(solution)/shard_map/fourier_terms/pallas_call | solution.py:135
  3.3 13.9 %all_to_all.5 = f32[32,1,64]{2,1,0:T(1,128)S(1)} all-to-all(f32[32,1,64]{2,1,0:T(1,128)S(1)} %bitcast.9), channel_id=1, replica_groups=mesh['sim'=16,'lens'=2] {'sim','lens'}, dimensions={0} | all-to-all | bytes 16384 | tf_op jit(solution)/shard_map/all_to_all | solution.py:218
  17.2 0.0 collective-permute-done.refs_0_
  17.2 0.0 copy-done
  17.2 0.0 copy-done.1
  17.2 1.1 %finish.1 = (f32[2,2,16]{2,1,0:T(2,128)}, f32[2,2,16]{2,1,0:T(2,128)}) custom-call(f32[16,2,64]{2,1,0:T(2,128)S(1)} %bitcast.8, bf16[2,16,8192]{2,1,0:T(8,128)(2,1)S(1)} %copy-done, bf16[2,16,8192]{2,1,0:T(8,128)(2,1)S(1)} %copy-done.1, bf16[2,16,8192]{2,1,0:T(8,128)(2,1)S(1)} %collective-permute-done.refs_0_), custom_call_target="tpu_custom_call" | custom-call | flops 33554432 | bytes 1572864 | tf_op jit(solution)/shard_map/finish/pallas_call | solution.py:190
Async XLA Ops:
  0.6 16.6 %collective-permute-start = (bf16[2,16,8192]{2,1,0:T(8,128)(2,1)}, bf16[2,16,8192]{2,1,0:T(8,128)(2,1)S(1)}, u32[]{:S(2)}, u32[]{:S(2)}) collective-permute-start(bf16[2,16,8192]{2,1,0:T(8,128)(2,1)} %own_ref.1), channel_id=1, source_target_pairs={{0,1},{1,0},{2,3},{3,2},{4,5},{5,4},{6,7},{7,6},{8,9},{9,8},{10,11... | collective-permute-start | bytes 1572872 | tf_op jit(solution)/shard_map/ppermute | solution.py:212
  1.2 16.1 %copy-start = (bf16[2,16,8192]{2,1,0:T(8,128)(2,1)S(1)}, bf16[2,16,8192]{2,1,0:T(8,128)(2,1)}, u32[]{:S(2)}) copy-start(bf16[2,16,8192]{2,1,0:T(8,128)(2,1)} %own_ref.1) | copy-start | bytes 1572868
  1.2 16.1 %copy-start.1 = (bf16[2,16,8192]{2,1,0:T(8,128)(2,1)S(1)}, bf16[2,16,8192]{2,1,0:T(8,128)(2,1)}, u32[]{:S(2)}) copy-start(bf16[2,16,8192]{2,1,0:T(8,128)(2,1)} %spin_ref.1) | copy-start | bytes 1572868

commit v4 on v3

--- a/solution.py
+++ b/solution.py
@@ -38,8 +38,8 @@
 
 
 def terms_kernel(
-    scale, m_hbm, cycle_hbm, block_hbm, weight_hbm, patch_hbm, out_ref,
-    m_ref, cycle_ref, block_ref, weight_ref, patch_ref, small_sem, patch_sem
+    scale, m_hbm, cycle_hbm, block_hbm, weight_hbm, patch_hbm, own_hbm, spin_hbm,
+    out_ref, own_ref, spin_ref, m_ref, cycle_ref, block_ref, weight_ref, patch_ref, small_sem, patch_sem, panel_sem
 ):
     number, shells, bpx = patch_ref.shape
     orders = m_ref.shape[1]
@@ -67,6 +67,10 @@
     slot = (row % n_sim) * m_dev + row // n_sim
     for copy in small:
         copy.wait()
+    panels = [
+        pltpu.make_async_copy(source, target, panel_sem.at[i])
+        for i, (source, target) in enumerate(((own_hbm, own_ref), (spin_hbm, spin_ref)))
+    ]
     m_row = m_ref[...].astype(jnp.float32)
     m_col = jnp.sum(jnp.where(slot == iota(square, 1), m_row, 0.0), axis=1, keepdims=True)
     m_col = m_col.astype(jnp.int32)
@@ -89,6 +93,8 @@
         weight = jnp.where(lane == shell, weight_ref[0:1, shell : shell + 1] * scale, weight)
     turn_c, turn_s = turn_c * weight, turn_s * weight
     chosen = (iota((n_sim, rows), 0) == cycle).astype(jnp.bfloat16)
+    for copy in panels:
+        copy.start()
     large[0].wait()
     total = jnp.zeros((4 * orders, rows), jnp.float32)
     for first in range(0, parts, GROUP):
@@ -119,9 +125,13 @@
     value = jnp.concatenate(pieces, axis=1)
     for column in range(lax.axis_size("lens")):
         out_ref[:, column] = value
-
-
-def fourier_terms(patches, patch_cycle, patch_block, m_values, shell_weight, scale):
+    for copy in panels:
+        copy.wait()
+
+
+def fourier_terms(
+    patches, patch_cycle, patch_block, m_values, shell_weight, own, spin, scale
+):
     number, shells, bpx = patches.shape
     orders = m_values.shape[0]
     n_sim, n_lens = lax.axis_size("sim"), lax.axis_size("lens")
@@ -134,18 +144,23 @@
     width = orders // n_sim * 2 * n_sim
     return pl.pallas_call(
         lambda *refs: terms_kernel(scale, *refs),
-        out_shape=jax.ShapeDtypeStruct((n_sim, n_lens, width), jnp.float32),
-        in_specs=[pl.BlockSpec(memory_space=pltpu.HBM)] * 5,
-        out_specs=pl.BlockSpec(memory_space=pltpu.VMEM),
+        out_shape=(
+            jax.ShapeDtypeStruct((n_sim, n_lens, width), jnp.float32),
+            jax.ShapeDtypeStruct(own.shape, own.dtype),
+            jax.ShapeDtypeStruct(spin.shape, spin.dtype),
+        ),
+        in_specs=[pl.BlockSpec(memory_space=pltpu.HBM)] * 7,
+        out_specs=[pl.BlockSpec(memory_space=pltpu.VMEM)] * 3,
         scratch_shapes=[pltpu.VMEM(x.shape, x.dtype) for x in small]
         + [
             pltpu.VMEM(patches.shape, patches.dtype),
             pltpu.SemaphoreType.DMA((4,)),
             pltpu.SemaphoreType.DMA((PIECES,)),
+            pltpu.SemaphoreType.DMA((2,)),
         ],
         compiler_params=pltpu.CompilerParams(vmem_limit_bytes=48 << 20),
         name="fourier_terms",
-    )(*[pltpu.with_memory_space_constraint(x, pltpu.HBM) for x in small + [patches]])
+    )(*[pltpu.with_memory_space_constraint(x, pltpu.HBM) for x in small + [patches, own, spin]])
 
 
 def finish_kernel(terms_ref, own_ref, spin_ref, *refs):
@@ -213,10 +228,19 @@
 
     others = [swap(legendre_panel, step) for step in range(1, n_lens)]
     scale = 1.0 / math.sqrt(NPIX * n_sim * n_lens * lmax)
-    terms = fourier_terms(patches, patch_cycle, patch_block, m_values, shell_weight, scale)
+    terms, own, spin = fourier_terms(
+        patches,
+        patch_cycle,
+        patch_block,
+        m_values,
+        shell_weight,
+        legendre_panel,
+        spin2_panel,
+        scale,
+    )
     terms = terms.reshape(n_sim * n_lens, 1, -1)
     terms = lax.all_to_all(terms, axes, 0, 0, tiled=True)
-    return finish(terms.reshape(n_sim, n_lens, -1), legendre_panel, spin2_panel, others)
+    return finish(terms.reshape(n_sim, n_lens, -1), own, spin, others)
 
 
 def solution(mesh):

time: 18.5 us -> 18.4 us (level)
  transfers between devices with their start and end apart: 1 -> 1, of which waited for: 0 -> 0; matrix products, arithmetic and copies ran while one was open for 0% -> 0% of each run, Pallas kernels for 12% -> 11%
where the time goes in v4:
time: 18.4 us; the launch traced here: 18.2 us
  blocking collectives  13.9 us (76%)
  Pallas kernels  3.16 us (17%)
  between operations  0.64 us (3%)
  starting transfers between devices  0.52 us (3%)
    all_to_all x1, blocking collectives, on_device(): terms = lax.all_to_all(terms, axes, 0, 0, tiled=True)  13.9 us
    pallas_call x1, Pallas kernels, fourier_terms(): pl.pallas_call(lambda *refs: terms_kernel(scale, *refs), out_shape=(jax.S...  2.06 us
    pallas_call x1, Pallas kernels, finish(): pl.pallas_call(finish_kernel, out_shape=(shape, shape), compiler_params=p...  1.1 us
    ppermute x1, starting transfers between devices, swap(): return lax.ppermute(x, axes, [(i, i ^ mask) for i in range(n_sim * n_lens)])  0.52 us
  transfers between devices with their start and end apart: 1, of which 0 were waited for; matrix products, arithmetic and copies ran while one was open for 0% of the time, Pallas kernels for 11%

profile of v4, /device:TPU:0, one launch (start us, length us, event | category | flops | bytes accessed | tf_op | source)
XLA Modules:
  0.0 18.2 jit_solution(2669071915513221243)
XLA Ops:
  0.6 0.5 %collective-permute-start = (bf16[2,16,8192]{2,1,0:T(8,128)(2,1)}, bf16[2,16,8192]{2,1,0:T(8,128)(2,1)S(1)}, u32[]{:S(2)}, u32[]{:S(2)}) collective-permute-start(bf16[2,16,8192]{2,1,0:T(8,128)(2,1)} %refs_5_.1), channel_id=1, source_target_pairs={{0,1},{1,0},{2,3},{3,2},{4,5},{5,4},{6,7},{7,6},{8,9},{9,8},{10,11... | collective-permute-start | bytes 1572872 | tf_op jit(solution)/shard_map/ppermute | solution.py:227
  1.2 2.1 %fourier_terms.1 = (f32[16,2,64]{2,1,0:T(2,128)S(1)}, bf16[2,16,8192]{2,1,0:T(8,128)(2,1)S(1)}, bf16[2,16,8192]{2,1,0:T(8,128)(2,1)S(1)}) custom-call(s32[1,32]{1,0:T(1,128)} %bitcast.10, s32[1,128]{1,0:T(1,128)} %bitcast.11, s32[1,128]{1,0:T(1,128)} %bitcast.12, f32[1,2]{1,0:T(1,128)} %bitcast.13, bf16[128,2,2048]{2,1,0:T(2,128)(2,1)} %refs_4_.1, ...), custom_call_target="tpu_custom_call" | custom-call | tf_op jit(solution)/shard_map/fourier_terms/pallas_call | solution.py:145
  3.2 13.9 %all_to_all.5 = f32[32,1,64]{2,1,0:T(1,128)S(1)} all-to-all(f32[32,1,64]{2,1,0:T(1,128)S(1)} %bitcast.9), channel_id=1, replica_groups=mesh['sim'=16,'lens'=2] {'sim','lens'}, dimensions={0} | all-to-all | bytes 16384 | tf_op jit(solution)/shard_map/all_to_all | solution.py:242
  17.1 0.0 collective-permute-done.refs_0_
  17.1 1.1 %finish.1 = (f32[2,2,16]{2,1,0:T(2,128)}, f32[2,2,16]{2,1,0:T(2,128)}) custom-call(f32[16,2,64]{2,1,0:T(2,128)S(1)} %bitcast.8, bf16[2,16,8192]{2,1,0:T(8,128)(2,1)S(1)} %get-tuple-element.6.own_ref, bf16[2,16,8192]{2,1,0:T(8,128)(2,1)S(1)} %get-tuple-element.7.spin_ref, bf16[2,16,8192]{2,1,0:T(8,128)(2,1)S(1)} %collective-permute-done.refs_0_), custom_call_target="tpu_custom_call" | custom-call | flops 33554432 | bytes 1572864 | tf_op jit(solution)/shard_map/finish/pallas_call | solution.py:205
Async XLA Ops:
  0.6 16.5 %collective-permute-start = (bf16[2,16,8192]{2,1,0:T(8,128)(2,1)}, bf16[2,16,8192]{2,1,0:T(8,128)(2,1)S(1)}, u32[]{:S(2)}, u32[]{:S(2)}) collective-permute-start(bf16[2,16,8192]{2,1,0:T(8,128)(2,1)} %refs_5_.1), channel_id=1, source_target_pairs={{0,1},{1,0},{2,3},{3,2},{4,5},{5,4},{6,7},{7,6},{8,9},{9,8},{10,11... | collective-permute-start | bytes 1572872 | tf_op jit(solution)/shard_map/ppermute | solution.py:227

commit v5 on v4

--- a/solution.py
+++ b/solution.py
@@ -39,7 +39,7 @@
 
 def terms_kernel(
     scale, m_hbm, cycle_hbm, block_hbm, weight_hbm, patch_hbm, own_hbm, spin_hbm,
-    out_ref, own_ref, spin_ref, m_ref, cycle_ref, block_ref, weight_ref, patch_ref, small_sem, patch_sem, panel_sem
+    out_ref, own_ref, spin_ref, factor_ref, m_ref, cycle_ref, block_ref, weight_ref, patch_ref, small_sem, patch_sem, panel_sem
 ):
     number, shells, bpx = patch_ref.shape
     orders = m_ref.shape[1]
@@ -62,6 +62,9 @@
     ]
     for copy in small + large:
         copy.start()
+    ell = iota(factor_ref.shape, 1).astype(jnp.float32)
+    below = jnp.sqrt(1.0 - 2.0 / jnp.maximum(ell * (ell + 1.0), 2.0))
+    factor_ref[...] = jnp.where(ell >= 2.0, below, 0.0)
     square = (orders, orders)
     row = iota(square, 0)
     slot = (row % n_sim) * m_dev + row // n_sim
@@ -148,9 +151,10 @@
             jax.ShapeDtypeStruct((n_sim, n_lens, width), jnp.float32),
             jax.ShapeDtypeStruct(own.shape, own.dtype),
             jax.ShapeDtypeStruct(spin.shape, spin.dtype),
+            jax.ShapeDtypeStruct((8, own.shape[2]), jnp.float32),
         ),
         in_specs=[pl.BlockSpec(memory_space=pltpu.HBM)] * 7,
-        out_specs=[pl.BlockSpec(memory_space=pltpu.VMEM)] * 3,
+        out_specs=[pl.BlockSpec(memory_space=pltpu.VMEM)] * 4,
         scratch_shapes=[pltpu.VMEM(x.shape, x.dtype) for x in small]
         + [
             pltpu.VMEM(patches.shape, patches.dtype),
@@ -163,56 +167,75 @@
     )(*[pltpu.with_memory_space_constraint(x, pltpu.HBM) for x in small + [patches, own, spin]])
 
 
-def finish_kernel(terms_ref, own_ref, spin_ref, *refs):
-    other_refs, (kappa_ref, shear_ref) = refs[:-2], refs[-2:]
+def make_grams(factor_ref, own_ref, spin_ref, other_refs, gram_ref):
+    for slot in range(own_ref.shape[0]):
+        shear = (spin_ref[slot].astype(jnp.float32) * factor_ref[0:1]).astype(jnp.bfloat16)
+        left = jnp.concatenate([own_ref[slot], shear], axis=0)
+        right = jnp.concatenate([own_ref[slot]] + [r[slot] for r in other_refs], axis=0)
+        gram_ref[slot] = lax.dot_general(right, left, NT, preferred_element_type=jnp.float32)
+
+
+def waits_longest():
+    return lax.axis_index("sim") == 0
+
+
+def gram_kernel(factor_ref, own_ref, spin_ref, *refs):
+    @pl.when(waits_longest())
+    def _():
+        make_grams(factor_ref, own_ref, spin_ref, refs[:-1], refs[-1])
+
+
+def finish_kernel(terms_ref, ahead_ref, factor_ref, own_ref, spin_ref, *refs):
+    other_refs, (kappa_ref, shear_ref, gram_ref) = refs[:-3], refs[-3:]
     m_dev, rows, lmax = own_ref.shape
     n_lens = lax.axis_size("lens")
     rank = lax.axis_index("lens")
-    ell = iota((8, lmax), 1).astype(jnp.float32)
-    factor = jnp.where(
-        ell >= 2.0, jnp.sqrt(1.0 - 2.0 / jnp.maximum(ell * (ell + 1.0), 2.0)), 0.0
-    )[0:1]
     steps = range(n_lens)
+
+    @pl.when(waits_longest())
+    def _():
+        gram_ref[...] = ahead_ref[...]
+
+    @pl.when(jnp.logical_not(waits_longest()))
+    def _():
+        make_grams(factor_ref, own_ref, spin_ref, other_refs, gram_ref)
+
     modes = [jnp.sum(terms_ref[:, rank ^ step], axis=0, keepdims=True) for step in steps]
-    same = iota((rows, rows), 0) == iota((rows, rows), 1)
+    turned = [jnp.broadcast_to(m, (8, m.shape[1])).T for m in modes]
     for slot in range(m_dev):
-        columns = []
+        gram = gram_ref[slot]
         for part in range(2):
             at = (slot * 2 + part) * rows
-            columns.append(
-                jnp.concatenate(
-                    [
-                        jnp.sum(jnp.where(same, m[:, at : at + rows], 0.0), axis=1, keepdims=True)
-                        for m in modes
-                    ],
-                    axis=0,
-                )
-            )
-        shear = (spin_ref[slot].astype(jnp.float32) * factor).astype(jnp.bfloat16)
-        left = jnp.concatenate([own_ref[slot], shear], axis=0)
-        right = jnp.concatenate([own_ref[slot]] + [r[slot] for r in other_refs], axis=0)
-        gram = lax.dot_general(right, left, NT, preferred_element_type=jnp.float32)
-        for part in range(2):
-            both = jnp.sum(gram * columns[part], axis=0, keepdims=True)
+            column = jnp.concatenate([t[at : at + rows, 0:1] for t in turned], axis=0)
+            both = jnp.sum(gram * column, axis=0, keepdims=True)
             kappa_ref[slot, part : part + 1] = both[:, :rows]
             shear_ref[slot, part : part + 1] = both[:, rows:]
 
 
-def finish(terms, own, spin, others):
+def gram_shape(own, others):
+    m_dev, rows, _ = own.shape
+    return m_dev, rows * (1 + len(others)), 2 * rows
+
+
+def grams_ahead(factor, own, spin, others):
+    return pl.pallas_call(
+        gram_kernel,
+        out_shape=jax.ShapeDtypeStruct(gram_shape(own, others), jnp.float32),
+        compiler_params=pltpu.CompilerParams(vmem_limit_bytes=48 << 20),
+        name="grams_ahead",
+    )(factor, own, spin, *others)
+
+
+def finish(terms, grams, factor, own, spin, others):
     m_dev, rows, lmax = own.shape
     shape = jax.ShapeDtypeStruct((m_dev, 2, rows), jnp.float32)
-    cycles = rows * (1 + len(others))
     return pl.pallas_call(
         finish_kernel,
         out_shape=(shape, shape),
+        scratch_shapes=[pltpu.VMEM(gram_shape(own, others), jnp.float32)],
         compiler_params=pltpu.CompilerParams(vmem_limit_bytes=48 << 20),
-        cost_estimate=pl.CostEstimate(
-            flops=4 * m_dev * rows * cycles * lmax,
-            bytes_accessed=2 * own.size * (2 + len(others)),
-            transcendentals=0,
-        ),
         name="finish",
-    )(terms, own, spin, *others)
+    )(terms, grams, factor, own, spin, *others)
 
 
 def on_device(
@@ -228,7 +251,7 @@
 
     others = [swap(legendre_panel, step) for step in range(1, n_lens)]
     scale = 1.0 / math.sqrt(NPIX * n_sim * n_lens * lmax)
-    terms, own, spin = fourier_terms(
+    terms, own, spin, factor = fourier_terms(
         patches,
         patch_cycle,
         patch_block,
@@ -238,9 +261,11 @@
         spin2_panel,
         scale,
     )
+    grams = grams_ahead(factor, own, spin, others)
+    terms, grams = lax.optimization_barrier((terms, grams))
     terms = terms.reshape(n_sim * n_lens, 1, -1)
     terms = lax.all_to_all(terms, axes, 0, 0, tiled=True)
-    return finish(terms.reshape(n_sim, n_lens, -1), own, spin, others)
+    return finish(terms.reshape(n_sim, n_lens, -1), grams, factor, own, spin, others)
 
 
 def solution(mesh):

time: 18.4 us -> 18.2 us (0.989)
  blocking collectives: 13.9 us -> 13.5 us
    all_to_all x1, blocking collectives: 13.9 us -> 13.5 us  [on_device(): terms = lax.all_to_all(terms, axes, 0, 0, tiled=True)]
    pallas_call x1 -> x2, Pallas kernels: 1.1 us -> 1.27 us  [the longest x1 0.85 us: finish(): pl.pallas_call(finish_kernel, out_shape=(shape, shape), scratch_shapes=[p...]
where the time goes in v5:
time: 18.2 us; the launch traced here: 18 us
  blocking collectives  13.5 us (74%)
  Pallas kernels  3.33 us (18%)
  between operations  0.65 us (4%)
  starting transfers between devices  0.52 us (3%)
    all_to_all x1, blocking collectives, on_device(): terms = lax.all_to_all(terms, axes, 0, 0, tiled=True)  13.5 us
    pallas_call x1, Pallas kernels, fourier_terms(): pl.pallas_call(lambda *refs: terms_kernel(scale, *refs), out_shape=(jax.S...  2.06 us
    pallas_call x1, Pallas kernels, finish(): pl.pallas_call(finish_kernel, out_shape=(shape, shape), scratch_shapes=[p...  0.85 us
    ppermute x1, starting transfers between devices, swap(): return lax.ppermute(x, axes, [(i, i ^ mask) for i in range(n_sim * n_lens)])  0.52 us
    pallas_call x1, Pallas kernels, grams_ahead(): pl.pallas_call(gram_kernel, out_shape=jax.ShapeDtypeStruct(gram_shape(own...  0.42 us
  transfers between devices with their start and end apart: 1, of which 0 were waited for; matrix products, arithmetic and copies ran while one was open for 0% of the time, Pallas kernels for 11%

profile of v5, /device:TPU:0, one launch (start us, length us, event | category | flops | bytes accessed | tf_op | source)
XLA Modules:
  0.0 18.0 jit_solution(336689031684736003)
XLA Ops:
  0.6 0.5 %collective-permute-start = (bf16[2,16,8192]{2,1,0:T(8,128)(2,1)}, bf16[2,16,8192]{2,1,0:T(8,128)(2,1)S(1)}, u32[]{:S(2)}, u32[]{:S(2)}) collective-permute-start(bf16[2,16,8192]{2,1,0:T(8,128)(2,1)} %refs_5_.1), channel_id=1, source_target_pairs={{0,1},{1,0},{2,3},{3,2},{4,5},{5,4},{6,7},{7,6},{8,9},{9,8},{10,11... | collective-permute-start | bytes 1572872 | tf_op jit(solution)/shard_map/ppermute | solution.py:250
  1.1 2.1 %fourier_terms.1 = (f32[16,2,64]{2,1,0:T(2,128)S(1)}, bf16[2,16,8192]{2,1,0:T(8,128)(2,1)S(1)}, bf16[2,16,8192]{2,1,0:T(8,128)(2,1)S(1)}, f32[8,8192]{1,0:T(8,128)S(1)}) custom-call(s32[1,32]{1,0:T(1,128)} %bitcast.10, s32[1,128]{1,0:T(1,128)} %bitcast.11, s32[1,128]{1,0:T(1,128)} %bitcast.12, f32[1,2]{1,0:T(1,128)} %bitcast.13, ...), custom_call_target="tpu_custom_call" | custom-call | tf_op jit(solution)/shard_map/fourier_terms/pallas_call | solution.py:148
  3.2 0.0 collective-permute-done.refs_0_
  3.2 0.4 %grams_ahead.1.ahead_ref = f32[2,32,32]{2,1,0:T(8,128)S(1)} custom-call(f32[8,8192]{1,0:T(8,128)S(1)} %get-tuple-element.9.factor_ref, bf16[2,16,8192]{2,1,0:T(8,128)(2,1)S(1)} %get-tuple-element.10.own_ref, bf16[2,16,8192]{2,1,0:T(8,128)(2,1)S(1)} %get-tuple-element.11.spin_ref, bf16[2,16,8192]{2,1,0:T(8,128)(2,1)S(1)} %collective-permute-done.refs_0_), custom_call_target="tpu_custom_call" | custom-call | tf_op jit(solution)/shard_map/grams_ahead/pallas_call | solution.py:221
  3.6 13.5 %all_to_all.5 = f32[32,1,64]{2,1,0:T(1,128)S(1)} all-to-all(f32[32,1,64]{2,1,0:T(1,128)S(1)} %bitcast.9), channel_id=1, replica_groups=mesh['sim'=16,'lens'=2] {'sim','lens'}, dimensions={0} | all-to-all | bytes 16384 | tf_op jit(solution)/shard_map/all_to_all | solution.py:267
  17.2 0.9 %finish.1 = (f32[2,2,16]{2,1,0:T(2,128)}, f32[2,2,16]{2,1,0:T(2,128)}) custom-call(f32[16,2,64]{2,1,0:T(2,128)S(1)} %bitcast.8, f32[2,32,32]{2,1,0:T(8,128)S(1)} %grams_ahead.1.ahead_ref, f32[8,8192]{1,0:T(8,128)S(1)} %get-tuple-element.9.factor_ref, bf16[2,16,8192]{2,1,0:T(8,128)(2,1)S(1)} %get-tuple-element.10.own_ref, ...), custom_call_target="tpu_custom_call" | custom-call | tf_op jit(solution)/shard_map/finish/pallas_call | solution.py:232
Async XLA Ops:
  0.6 2.6 %collective-permute-start = (bf16[2,16,8192]{2,1,0:T(8,128)(2,1)}, bf16[2,16,8192]{2,1,0:T(8,128)(2,1)S(1)}, u32[]{:S(2)}, u32[]{:S(2)}) collective-permute-start(bf16[2,16,8192]{2,1,0:T(8,128)(2,1)} %refs_5_.1), channel_id=1, source_target_pairs={{0,1},{1,0},{2,3},{3,2},{4,5},{5,4},{6,7},{7,6},{8,9},{9,8},{10,11... | collective-permute-start | bytes 1572872 | tf_op jit(solution)/shard_map/ppermute | solution.py:250
